TPU v7x, 32 devices: a whole 2x2x4 slice. The times are simulated.
32 devices in a mesh: dp: 8 (over z, x), expert: 2 (over core), ffn: 2 (over y).
Axes of the slice: x: 2, y: 2, z: 4, core: 2. Of those that a mesh axis runs over, the one named last changes fastest.
Arguments:
- grad_rows: bfloat16 [1024, 6144], P('dp', 'ffn'), may hold values from -80 to 80
- gate_probs: float32 [1024, 2], P('dp'), may hold values from 0.1 to 1
- expert_ids: int32 [1024, 2], P('dp'), may hold values from 0 to 3, all different within a row; in each aligned block of 128 rows (0 to 127, 128 to 255, ...) at most 72 rows name the same one
- gate_pre: bfloat16 [4, 576, 8192], P('expert', 'ffn', 'dp'), may hold values from -6 to 6
- up_pre: bfloat16 [4, 576, 8192], P('expert', 'ffn', 'dp'), may hold values from -40 to 40
- down_weight: bfloat16 [4, 8192, 6144], P('expert', 'dp', 'ffn'), may hold values from -0.0625 to 0.0625
Outputs:
- down_grad: bfloat16 [4, 8192, 6144], P('expert', 'dp', 'ffn')
- gate_grad: bfloat16 [4, 576, 8192], P('expert', 'ffn', 'dp')
- up_grad: bfloat16 [4, 576, 8192], P('expert', 'ffn', 'dp')
Inputs may be any that keep to these rules, and one draw needn't show every extreme that they name: `expert_ids`: in the 128 tokens of one index of dp no expert is named by more than 72 routes, a bound that some block reaches; a token's two routes name different experts.
All inputs are finite; a program needn't handle non-finite values.
Results may differ from a plain program's by a relative error of at most 0.019.
Values may be sent and summed in bfloat16 or wider, within the bound.
A program may use at most 128 MiB of HBM per device.

v0:
```python
import math

import jax
import jax.numpy as jnp
from jax import lax
from jax.sharding import PartitionSpec as P

CAP = 72


def slot_table(route_ids, experts_total):
    tokens_here, routes = route_ids.shape
    flat_ids = route_ids.reshape(tokens_here * routes)
    one_hot = (flat_ids[:, None] == jnp.arange(experts_total, dtype=jnp.int32)[None, :]).astype(
        jnp.int32
    )
    earlier = jnp.cumsum(one_hot, axis=0) - one_hot
    return jnp.sum(earlier * one_hot, axis=1).reshape(tokens_here, routes)


def on_device(grad_rows, gate_probs, expert_ids, gate_pre, up_pre, down_weight):
    experts_here, rows_here, hidden_width = gate_pre.shape
    feature_width = down_weight.shape[2]
    capacity = CAP
    experts_total = experts_here * lax.axis_size("expert")
    slot_index = slot_table(expert_ids, experts_total)
    first_expert = lax.axis_index("expert") * experts_here
    local_ids = expert_ids - first_expert
    expert_match = (
        local_ids[:, :, None] == jnp.arange(experts_here, dtype=jnp.int32)[None, None, :]
    ).astype(jnp.float32)
    expert_match = expert_match * gate_probs[:, :, None]
    slot_match = (
        slot_index[:, :, None] == jnp.arange(capacity, dtype=jnp.int32)[None, None, :]
    ).astype(jnp.float32)
    placing = jnp.einsum("tke,tks->est", expert_match, slot_match, precision=lax.Precision.HIGHEST)
    dispatched = jnp.einsum(
        "est,td->esd", placing, grad_rows.astype(jnp.float32), precision=lax.Precision.HIGHEST
    ).astype(jnp.bfloat16)
    arrived = lax.all_gather(dispatched, "dp", axis=1, tiled=True)
    gate_value = gate_pre.astype(jnp.float32)
    up_value = up_pre.astype(jnp.float32)
    sigmoid_gate = jax.nn.sigmoid(gate_value)
    silu_gate = gate_value * sigmoid_gate
    hidden = (silu_gate * up_value).astype(jnp.bfloat16)
    partial_sums = jnp.einsum(
        "erd,efd->erf", arrived, down_weight, preferred_element_type=jnp.float32
    )
    own_rows = lax.psum_scatter(
        partial_sums.astype(jnp.bfloat16), "ffn", scatter_dimension=1, tiled=True
    ).astype(jnp.float32)
    gate_grad = (
        own_rows * up_value * sigmoid_gate * (1.0 + gate_value * (1.0 - sigmoid_gate))
    ).astype(jnp.bfloat16)
    up_grad = (own_rows * silu_gate).astype(jnp.bfloat16)
    weight_grad = jnp.einsum(
        "erf,erd->efd",
        lax.all_gather(hidden, "ffn", axis=1, tiled=True),
        arrived,
        preferred_element_type=jnp.float32,
    )
    squares = lax.psum(jnp.sum(weight_grad * weight_grad), ("dp", "expert", "ffn"))
    entry_count = (
        float(experts_total)
        * float(hidden_width * lax.axis_size("dp"))
        * float(feature_width * lax.axis_size("ffn"))
    )
    clip_limit = jnp.float32(0.5 * math.sqrt(entry_count))
    factor = clip_limit / jnp.maximum(jnp.sqrt(squares), clip_limit)
    down_grad = (weight_grad * factor).astype(jnp.bfloat16)
    return (down_grad, gate_grad, up_grad)


def solution(mesh):
    placed = (
        P("dp", "ffn"),
        P("dp", None),
        P("dp", None),
        P("expert", "ffn", "dp"),
        P("expert", "ffn", "dp"),
        P("expert", "dp", "ffn"),
    )
    return jax.shard_map(
        on_device,
        mesh=mesh,
        in_specs=placed,
        out_specs=(P("expert", "dp", "ffn"), P("expert", "ffn", "dp"), P("expert", "ffn", "dp")),
        check_vma=False,
    )
```

profile of v0, /device:TPU:0, one launch (start us, length us, event | category | flops | bytes accessed | tf_op | source)
XLA Modules:
  0.0 295.8 jit_solution(15484222577021521856)
XLA Ops:
  7.2 0.0 copy-start
  7.2 0.0 all-gather.5.cloned.1.call-start
  7.2 0.8 copy.13
  8.1 0.1 eq.57
  8.2 0.1 eq.53
  8.4 0.7 broadcast_subtract_fusion
  9.1 0.1 copy.17
  9.2 1.2 reduce-window.6
  10.4 0.1 slice.8
  10.5 0.1 copy.15
  10.6 0.1 copy.16
  10.7 0.1 add_bitcast_fusion
  10.8 0.1 eq.61
  11.0 0.8 copy.18
  11.7 1.1 fusion.10
  12.9 0.1 copy.19
  13.0 0.0 copy-done
  13.0 1.8 convolution_convert_fusion
  14.7 0.0 all-gather.5.cloned.1.call-update
  14.8 0.0 reduce-scatter.2.cloned.1.call-start
  14.8 111.6 %all-gather.5.cloned.1.call-done = bf16[2,576,3072]{2,1,0:T(8,128)(2,1)} async-done(((bf16[2,72,3072]{2,1,0:T(8,128)(2,1)}), bf16[2,576,3072]{2,1,0:T(8,128)(2,1)}) %all-gather.5.cloned.1.call-update) | async-done | bytes 7077904 | tf_op jit(solution)/shard_map/all_gather | solution.py:40
  126.4 13.5 %convolution_convert_fusion.1 = bf16[2,576,1024]{2,1,0:T(8,128)(2,1)} fusion(bf16[2,576,3072]{2,1,0:T(8,128)(2,1)} %all-gather.5.cloned.1.call-done, bf16[2,1024,3072]{2,1,0:T(8,128)(2,1)} %param.11), kind=kOutput, calls=%fused_computation.18 | convolution fusion | flops 7248936960 | bytes 22020096 | tf_op jit(solution)/shard_map/erd,efd->erf/dot_general | solution.py:46
  139.9 0.0 copy-start.2
  140.0 0.0 copy-start.3
  140.0 0.0 reduce-scatter.2.cloned.1.call-update
  140.0 0.2 all-gather.3.cloned.1.call-start
  140.2 32.8 %reduce-scatter.2.cloned.1.call-done = bf16[2,288,1024]{2,1,0:T(8,128)(2,1)} async-done(((bf16[2,576,1024]{2,1,0:T(8,128)(2,1)}), bf16[2,288,1024]{2,1,0:T(8,128)(2,1)}) %reduce-scatter.2.cloned.1.call-update) | async-done | bytes 1179664 | tf_op jit(solution)/shard_map/reduce_scatter | solution.py:49
  173.0 0.0 copy-done.2
  173.0 0.0 copy-done.3
  173.0 5.2 %fusion.4 = (bf16[2,288,1024]{2,1,0:T(8,128)(2,1)}, bf16[2,288,1024]{2,1,0:T(8,128)(2,1)}, bf16[2,288,1024]{2,1,0:T(8,128)(2,1)}) fusion(bf16[2,288,1024]{2,1,0:T(8,128)(2,1)} %reduce-scatter.2.cloned.1.call-done, bf16[2,288,1024]{2,1,0:T(8,128)(2,1)S(1)} %copy-done.2, bf16[2,288,1024]{2,1,0:T(8,128)(2,1)S(1)} %copy-done.3), kind=kLoop, calls=%fused_computation.13 | loop fusion | flops 10616832 | bytes 7077888 | tf_op jit(solution)/shard_map/convert_element_type | solution.py:55
  178.2 0.0 all-gather.3.cloned.1.call-update
  178.3 36.2 %all-gather.3.cloned.1.call-done = bf16[2,576,1024]{2,1,0:T(8,128)(2,1)} async-done(((bf16[2,288,1024]{2,1,0:T(8,128)(2,1)}), bf16[2,576,1024]{2,1,0:T(8,128)(2,1)}) %all-gather.3.cloned.1.call-update) | async-done | bytes 2359312 | tf_op jit(solution)/shard_map/all_gather | solution.py:58
  214.5 20.4 %multiply_reduce_fusion = (f32[]{:T(128)}, f32[2,1024,3072]{2,1,0:T(8,128)}) fusion(bf16[2,576,1024]{2,1,0:T(8,128)(2,1)} %all-gather.3.cloned.1.call-done, bf16[2,576,3072]{2,1,0:T(8,128)(2,1)} %all-gather.5.cloned.1.call-done), kind=kOutput, calls=%fused_computation.1 | convolution fusion | flops 7260340224 | bytes 34603012 | tf_op jit(solution)/shard_map/erf,erd->efd/dot_general | solution.py:56
  234.9 39.5 %psum.7 = f32[]{:T(128)} all-reduce(f32[]{:T(128)} %get-tuple-element.6), channel_id=1, replica_groups=mesh['dp'=8,'expert'=2,'ffn'=2] {'dp','expert','ffn'}, use_global_device_ids=true, to_apply=%region_4.5 | all-reduce | flops 1 | bytes 8 | tf_op jit(solution)/shard_map/psum | solution.py:62
  275.2 0.0 copy-start.1
  275.2 14.1 %multiply_convert_fusion = bf16[2,1024,3072]{2,1,0:T(8,128)(2,1)} fusion(f32[2,1024,3072]{2,1,0:T(8,128)} %get-tuple-element.7, f32[]{:T(128)S(6)} %div.7), kind=kLoop, calls=%fused_computation | loop fusion | flops 12582912 | bytes 37748740 | tf_op jit(solution)/shard_map/convert_element_type | solution.py:70
  289.3 0.0 copy-done.1
  (4 shorter events, 0.1 us)
Async XLA Ops:
  7.2 5.8 %copy-start = (bf16[128,3072]{1,0:T(8,128)(2,1)S(1)}, bf16[128,3072]{1,0:T(8,128)(2,1)}, u32[]{:S(2)}) copy-start(bf16[128,3072]{1,0:T(8,128)(2,1)} %param.6) | copy-start | bytes 2359300
  7.2 119.2 %all-gather.5.cloned.1.call-start = ((), (), s32[]{:S(2)}) async-start(), calls=%async_computation.2 | async-start | bytes 7962624 | tf_op jit(solution)/shard_map/all_gather | solution.py:40
  14.8 158.3 %reduce-scatter.2.cloned.1.call-start = ((), (), s32[]{:S(2)}) async-start(), calls=%async_computation.3 | async-start | bytes 3538944 | tf_op jit(solution)/shard_map/reduce_scatter | solution.py:49
  139.9 33.1 %copy-start.2 = (bf16[2,288,1024]{2,1,0:T(8,128)(2,1)S(1)}, bf16[2,288,1024]{2,1,0:T(8,128)(2,1)}, u32[]{:S(2)}) copy-start(bf16[2,288,1024]{2,1,0:T(8,128)(2,1)} %param.9) | copy-start | bytes 3538948
  140.0 33.1 %copy-start.3 = (bf16[2,288,1024]{2,1,0:T(8,128)(2,1)S(1)}, bf16[2,288,1024]{2,1,0:T(8,128)(2,1)}, u32[]{:S(2)}) copy-start(bf16[2,288,1024]{2,1,0:T(8,128)(2,1)} %param.10) | copy-start | bytes 3538948
  140.0 74.5 %all-gather.3.cloned.1.call-start = ((), (), s32[]{:S(2)}) async-start(), calls=%async_computation.1 | async-start | bytes 3538944 | tf_op jit(solution)/shard_map/all_gather | solution.py:58
  275.2 14.2 %copy-start.1 = (bf16[128,3072]{1,0:T(8,128)(2,1)S(1)}, bf16[128,3072]{1,0:T(8,128)(2,1)}, u32[]{:S(2)}) copy-start(bf16[128,3072]{1,0:T(8,128)(2,1)} %param.6) | copy-start | bytes 2359300
Sparse Core Ops, SparseCore 0:
  14.9 111.4 all-gather.4
  140.1 32.8 reduce-scatter.1
  178.4 36.0 all-gather.2
where the time goes:
time: 296 us
  waiting for transfers between devices  181 us (61%)
  blocking collectives  39.5 us (13%)
  matrix products  36.8 us (12%)
  other arithmetic  21.4 us (7%)
  between operations  14.5 us (5%)
    all_gather x1, waiting for transfers between devices, on_device(): arrived = lax.all_gather(dispatched, 'dp', axis=1, tiled=True)  112 us
    psum x1, blocking collectives, on_device(): lax.psum(jnp.sum(weight_grad * weight_grad), ('dp', 'expert', 'ffn'))  39.5 us
    all_gather x1, waiting for transfers between devices, on_device(): lax.all_gather(hidden, 'ffn', axis=1, tiled=True)  36.2 us
    reduce_scatter x1, waiting for transfers between devices, on_device(): lax.psum_scatter(partial_sums.astype(jnp.bfloat16), 'ffn', scatter_dimens...  32.8 us
    dot_general x1, matrix products, on_device(): jnp.einsum('erf,erd->efd', lax.all_gather(hidden, 'ffn', axis=1, tiled=Tr...  20.4 us
    convert_element_type x1, other arithmetic, on_device(): down_grad = (weight_grad * factor).astype(jnp.bfloat16)  14.1 us
    dot_general x1, matrix products, on_device(): jnp.einsum('erd,efd->erf', arrived, down_weight, preferred_element_type=j...  13.5 us
  transfers between devices with their start and end apart: 3, of which 3 were waited for; matrix products, arithmetic and copies ran while one was open for 0% of the time, Pallas kernels for 0%

commit v1 on v0

--- a/solution.py
+++ b/solution.py
@@ -1,11 +1,17 @@
+import functools
 import math
 
 import jax
 import jax.numpy as jnp
 from jax import lax
+from jax.experimental import pallas as pl
+from jax.experimental.pallas import tpu as pltpu
 from jax.sharding import PartitionSpec as P
 
 CAP = 72
+MESH = pl.DeviceIdType.MESH
+F32 = jnp.float32
+BF16 = jnp.bfloat16
 
 
 def slot_table(route_ids, experts_total):
@@ -71,6 +77,424 @@
     return (down_grad, gate_grad, up_grad)
 
 
+def fused_kernel(
+    n_dp, meta_ref, rows_ref, gate_ref, up_ref, weight_ref,
+    wide_ref, gate_out, up_out, norm_ref,
+    tokens, metas, placed, weight, hidden, hidden_t, mine, outgoing, incoming,
+    squares, norm_dp, norm_core, norm_pair, own_norm,
+    load_sem, meta_send, meta_recv, z_send, z_recv, x_send, x_recv, core_send, core_recv,
+    hidden_send, hidden_recv, part_send, part_recv, norm_send, norm_recv, wide_sem,
+):
+    dp = lax.axis_index("dp")
+    core = lax.axis_index("expert")
+    side = lax.axis_index("ffn")
+    n_z = n_dp // 2
+    z, x = dp // 2, dp % 2
+    experts, own_slots, units = gate_ref.shape
+    block = rows_ref.shape[0]
+    half = block // 2
+    width = rows_ref.shape[1]
+    group = 2 * CAP
+    groups_own = n_z // 2
+
+    load_rows = pltpu.make_async_copy(
+        rows_ref, tokens.at[z, pl.ds(pl.multiple_of(x * block, block), block), :], load_sem.at[0]
+    )
+    load_rows.start()
+    load_weight = pltpu.make_async_copy(weight_ref, weight, load_sem.at[1])
+    load_weight.start()
+
+    barrier = pltpu.get_barrier_semaphore()
+    for step in range(1, n_dp):
+        pl.semaphore_signal(
+            barrier, inc=1, device_id={"dp": (dp + step) % n_dp}, device_id_type=MESH
+        )
+    pl.semaphore_signal(barrier, inc=1, device_id={"expert": 1 - core}, device_id_type=MESH)
+    pl.semaphore_signal(barrier, inc=1, device_id={"ffn": 1 - side}, device_id_type=MESH)
+    pl.semaphore_wait(barrier, n_dp + 1)
+
+    def half_rows(z_of, x_of, core_of):
+        start = pl.multiple_of(x_of * block + core_of * half, half)
+        return tokens.at[z_of, pl.ds(start, half), :]
+
+    def remote(src, dst, send, recv, to):
+        return pltpu.make_async_remote_copy(
+            src_ref=src, dst_ref=dst, send_sem=send, recv_sem=recv,
+            device_id=to, device_id_type=MESH,
+        )
+
+    def z_copy(g, up):
+        place = half_rows(g, x, core)
+        to = jnp.clip(z + (1 if up else -1), 0, n_z - 1) * 2 + x
+        return remote(place, place, z_send.at[1 if up else 0, g], z_recv.at[g], {"dp": to})
+
+    def x_copy(g, x_of):
+        place = half_rows(g, x_of, core)
+        return remote(place, place, x_send.at[g], x_recv.at[g], {"dp": z * 2 + 1 - x})
+
+    def core_copy(g, x_of, core_of):
+        place = half_rows(g, x_of, core_of)
+        return remote(
+            place, place, core_send.at[g, x_of], core_recv.at[g, x_of], {"expert": 1 - core}
+        )
+
+    def meta_copy(step, source):
+        return remote(
+            metas.at[source], metas.at[source], meta_send.at[step], meta_recv.at[step],
+            {"dp": (dp + step) % n_dp},
+        )
+
+    metas[dp] = meta_ref[...]
+    for step in range(1, n_dp):
+        meta_copy(step, dp).start()
+    load_rows.wait()
+
+    @pl.when(z < n_z - 1)
+    def _():
+        z_copy(z, True).start()
+
+    @pl.when(z > 0)
+    def _():
+        z_copy(z, False).start()
+
+    x_copy(z, x).start()
+
+    def hidden_copy(e, side_of):
+        start = pl.multiple_of(side_of * own_slots, 16)
+        place = hidden.at[e, pl.ds(start, own_slots), :]
+        return remote(place, place, hidden_send.at[e], hidden_recv.at[e], {"ffn": 1 - side})
+
+    piece = 48
+    for e in range(experts):
+
+        def hidden_piece(i, carry):
+            start = pl.multiple_of(i * piece, 16)
+            gate = gate_ref[e, pl.ds(start, piece), :].astype(F32)
+            up = up_ref[e, pl.ds(start, piece), :].astype(F32)
+            to = pl.multiple_of(side * own_slots + start, 16)
+            hidden[e, pl.ds(to, piece), :] = (gate * jax.nn.sigmoid(gate) * up).astype(BF16)
+            return carry
+
+        lax.fori_loop(0, own_slots // piece, hidden_piece, 0)
+        hidden_copy(e, side).start()
+
+    for step in range(1, n_dp):
+        meta_copy(step, (dp - step + n_dp) % n_dp).wait_recv()
+    load_weight.wait()
+
+    first = (core * experts).astype(F32)
+    n_cols = 4
+    cols = width // n_cols
+    unit_cols = 256
+
+    def part_copy(index, e):
+        return remote(
+            outgoing.at[index, e], incoming.at[index, e], part_send.at[index, e],
+            part_recv.at[index, e], {"ffn": 1 - side},
+        )
+
+    def process(g):
+        meta = jnp.concatenate([metas[2 * g], metas[2 * g + 1]], axis=1)
+        lane = lax.broadcasted_iota(jnp.int32, (2 * block, 2 * block), 1)
+        sub = lax.broadcasted_iota(jnp.int32, (2 * block, 2 * block), 0)
+        before = jnp.where(
+            (sub < lane) & ((sub >= block) == (lane >= block)), 1.0, 0.0
+        ).astype(BF16)
+        row = lax.broadcasted_iota(jnp.int32, (group, 2 * block), 0).astype(F32)
+        offset = jnp.where(
+            lax.broadcasted_iota(jnp.int32, (1, 2 * block), 1) >= block, float(CAP), 0.0
+        )
+        start = pl.multiple_of(g * group, 16)
+        for e in range(experts):
+            first_match = meta[0:1] == first + e
+            second_match = meta[1:2] == first + e
+            match = jnp.where(first_match | second_match, 1.0, 0.0)
+            prob = jnp.where(first_match, meta[2:3], jnp.where(second_match, meta[3:4], 0.0))
+            earlier = jnp.dot(
+                jnp.broadcast_to(match, (16, 2 * block)).astype(BF16), before,
+                preferred_element_type=F32,
+            )[0:1]
+            key = jnp.where(match > 0.0, earlier + offset, -1.0)
+            chosen = row == key
+            scale = jnp.sum(jnp.where(chosen, prob, 0.0), axis=1, keepdims=True)
+            select = jnp.where(chosen, 1.0, 0.0).astype(BF16)
+
+            def place_cols(j, carry):
+                at = pl.ds(pl.multiple_of(j * cols, 128), cols)
+                picked = jnp.dot(select, tokens[g, :, at], preferred_element_type=F32)
+                placed[e, pl.ds(start, group), at] = (picked * scale).astype(BF16)
+                return carry
+
+            lax.fori_loop(0, n_cols, place_cols, 0)
+        is_own = (g // groups_own) == side
+        index = g % groups_own
+        for e in range(experts):
+
+            def unit_tile(j, carry):
+                at = pl.ds(pl.multiple_of(j * unit_cols, 128), unit_cols)
+                term = lax.dot_general(
+                    placed[e, pl.ds(start, group), :], weight[e, at, :],
+                    (((1,), (1,)), ((), ())), preferred_element_type=F32,
+                ).astype(BF16)
+
+                @pl.when(is_own)
+                def _():
+                    mine[index, e, :, at] = term
+
+                @pl.when(jnp.logical_not(is_own))
+                def _():
+                    outgoing[index, e, :, at] = term
+
+                return carry
+
+            lax.fori_loop(0, units // unit_cols, unit_tile, 0)
+
+            @pl.when(jnp.logical_not(is_own))
+            def _():
+                part_copy(index, e).start()
+
+    def stage(s, carry):
+        for sign in (-1, 1):
+            g = z + sign * (s + 1)
+            onward = z - sign
+
+            @pl.when((g >= 0) & (g < n_z))
+            def _():
+                z_copy(g, sign < 0).wait_recv()
+
+                @pl.when((onward >= 0) & (onward < n_z))
+                def _():
+                    z_copy(g, sign < 0).start()
+
+                x_copy(g, x).start()
+                core_copy(g, x, core).start()
+
+        for sign in (-1, 1):
+            g = z + sign * s
+
+            @pl.when((g >= 0) & (g < n_z) & ((s > 0) | (sign < 0)))
+            def _():
+                x_copy(g, 1 - x).wait_recv()
+                core_copy(g, 1 - x, core).start()
+
+        def side_of_stage(k, inner):
+            g = z + (2 * k - 1) * s
+
+            @pl.when((g >= 0) & (g < n_z) & ((s > 0) | (k == 0)))
+            def _():
+                @pl.when(s > 0)
+                def _():
+                    core_copy(g, x, 1 - core).wait_recv()
+
+                core_copy(g, 1 - x, 1 - core).wait_recv()
+                process(g)
+
+            return inner
+
+        lax.fori_loop(0, 2, side_of_stage, 0)
+        return carry
+
+    lax.fori_loop(0, n_z, stage, 0)
+
+    for e in range(experts):
+        hidden_copy(e, 1 - side).wait_recv()
+        hidden_copy(e, side).wait_send()
+    slots = hidden.shape[1]
+    for e in range(experts):
+
+        def turn(j, carry):
+            at = pl.ds(pl.multiple_of(j * 128, 128), 128)
+            hidden_t[e, at, :] = hidden[e, :, at].T
+            return carry
+
+        lax.fori_loop(0, units // 128, turn, 0)
+
+    squares[...] = jnp.zeros_like(squares)
+    tile = 256
+    tiles = width // tile
+
+    def wide_copy(e, j):
+        at = pl.ds(pl.multiple_of(j * tile, 128), tile)
+        return pltpu.make_async_copy(weight.at[e, :, at], wide_ref.at[e, :, at], wide_sem.at[e, j])
+
+    for e in range(experts):
+
+        def wide_tile(j, carry):
+            at = pl.ds(pl.multiple_of(j * tile, 128), tile)
+            product = jnp.dot(hidden_t[e], placed[e, :, at], preferred_element_type=F32)
+            weight[e, :, at] = product.astype(BF16)
+            squares[...] += jnp.sum((product * product).reshape(units // 8, 8, tile), axis=0)
+            wide_copy(e, j).start()
+            return carry
+
+        lax.fori_loop(0, tiles, wide_tile, 0)
+
+    own_norm[0] = squares[:, 0:128] + squares[:, 128:256]
+
+    def norm_copy(step, to_slot):
+        return remote(
+            own_norm.at[0], norm_dp.at[to_slot], norm_send.at[step], norm_recv.at[step],
+            {"dp": (dp + step) % n_dp},
+        )
+
+    for step in range(1, n_dp):
+        norm_copy(step, dp).start()
+    norm_dp[dp] = own_norm[0]
+    for step in range(1, n_dp):
+        norm_copy(step, (dp - step + n_dp) % n_dp).wait_recv()
+    total = norm_dp[0]
+    for i in range(1, n_dp):
+        total = total + norm_dp[i]
+    own_norm[1] = total
+    core_norm = remote(
+        own_norm.at[1], norm_core, norm_send.at[0], norm_recv.at[0], {"expert": 1 - core}
+    )
+    core_norm.start()
+    core_norm.wait()
+    own_norm[2] = total + norm_core[...]
+    pair_norm = remote(
+        own_norm.at[2], norm_pair, norm_send.at[n_dp], norm_recv.at[n_dp], {"ffn": 1 - side}
+    )
+    pair_norm.start()
+
+    for index in range(groups_own):
+        for e in range(experts):
+            part_copy(index, e).wait_recv()
+
+            def grad_piece(i, carry):
+                here = pl.multiple_of(i * piece, 16)
+                at = pl.ds(pl.multiple_of(index * group + here, 16), piece)
+                gate = gate_ref[e, at, :].astype(F32)
+                up = up_ref[e, at, :].astype(F32)
+                grad = (
+                    mine[index, e, pl.ds(here, piece), :].astype(F32)
+                    + incoming[index, e, pl.ds(here, piece), :].astype(F32)
+                )
+                sig = jax.nn.sigmoid(gate)
+                gate_out[e, at, :] = (grad * up * sig * (1.0 + gate * (1.0 - sig))).astype(BF16)
+                up_out[e, at, :] = (grad * (gate * sig)).astype(BF16)
+                return carry
+
+            lax.fori_loop(0, group // piece, grad_piece, 0)
+
+    pair_norm.wait()
+    norm_ref[...] = own_norm[2] + norm_pair[...]
+
+    for index in range(groups_own):
+        for e in range(experts):
+            part_copy(index, e).wait_send()
+    for step in range(1, n_dp):
+        meta_copy(step, dp).wait_send()
+        norm_copy(step, dp).wait_send()
+
+    def drain(g, carry):
+        @pl.when((z < n_z - 1) & (g <= z))
+        def _():
+            z_copy(g, True).wait_send()
+
+        @pl.when((z > 0) & (g >= z))
+        def _():
+            z_copy(g, False).wait_send()
+
+        x_copy(g, x).wait_send()
+
+        @pl.when(g != z)
+        def _():
+            core_copy(g, x, core).wait_send()
+
+        core_copy(g, 1 - x, core).wait_send()
+        return carry
+
+    lax.fori_loop(0, n_z, drain, 0)
+    for e in range(experts):
+
+        def wide_wait(j, carry):
+            wide_copy(e, j).wait()
+            return carry
+
+        lax.fori_loop(0, tiles, wide_wait, 0)
+
+
+def fused_call(n_dp, meta, grad_rows, gate_pre, up_pre, down_weight):
+    experts, own_slots, units = gate_pre.shape
+    block, width = grad_rows.shape
+    n_z = n_dp // 2
+    group = 2 * CAP
+    groups_own = n_z // 2
+    slots = n_dp * CAP
+    vmem = pl.BlockSpec(memory_space=pltpu.VMEM)
+    hbm = pl.BlockSpec(memory_space=pl.ANY)
+    dma = pltpu.SemaphoreType.DMA
+    return pl.pallas_call(
+        functools.partial(fused_kernel, n_dp),
+        out_shape=(
+            jax.ShapeDtypeStruct(down_weight.shape, BF16),
+            jax.ShapeDtypeStruct(gate_pre.shape, BF16),
+            jax.ShapeDtypeStruct(up_pre.shape, BF16),
+            jax.ShapeDtypeStruct((8, 128), F32),
+        ),
+        in_specs=[vmem, hbm, vmem, vmem, hbm],
+        out_specs=(hbm, vmem, vmem, vmem),
+        scratch_shapes=[
+            pltpu.VMEM((n_z, 2 * block, width), BF16),
+            pltpu.VMEM((n_dp, 8, block), F32),
+            pltpu.VMEM((experts, slots, width), BF16),
+            pltpu.VMEM(down_weight.shape, BF16),
+            pltpu.VMEM((experts, slots, units), BF16),
+            pltpu.VMEM((experts, units, slots), BF16),
+            pltpu.VMEM((groups_own, experts, group, units), BF16),
+            pltpu.VMEM((groups_own, experts, group, units), BF16),
+            pltpu.VMEM((groups_own, experts, group, units), BF16),
+            pltpu.VMEM((8, 256), F32),
+            pltpu.VMEM((n_dp, 8, 128), F32),
+            pltpu.VMEM((8, 128), F32),
+            pltpu.VMEM((8, 128), F32),
+            pltpu.VMEM((3, 8, 128), F32),
+            dma((2,)),
+            dma((n_dp,)),
+            dma((n_dp,)),
+            dma((2, n_z)),
+            dma((n_z,)),
+            dma((n_z,)),
+            dma((n_z,)),
+            dma((n_z, 2)),
+            dma((n_z, 2)),
+            dma((experts,)),
+            dma((experts,)),
+            dma((groups_own, experts)),
+            dma((groups_own, experts)),
+            dma((n_dp + 1,)),
+            dma((n_dp + 1,)),
+            dma((experts, width // 256)),
+        ],
+        compiler_params=pltpu.CompilerParams(
+            collective_id=0, has_side_effects=True, vmem_limit_bytes=58 * 1024 * 1024
+        ),
+    )(meta, grad_rows, gate_pre, up_pre, down_weight)
+
+
+def fused_device(grad_rows, gate_probs, expert_ids, gate_pre, up_pre, down_weight):
+    experts_here, rows_here, hidden_width = gate_pre.shape
+    feature_width = down_weight.shape[2]
+    n_dp = lax.axis_size("dp")
+    meta = jnp.concatenate(
+        [expert_ids.astype(F32), gate_probs, jnp.zeros((expert_ids.shape[0], 4), F32)], axis=1
+    ).T
+    wide, gate_grad, up_grad, norm = fused_call(
+        n_dp, meta, grad_rows, gate_pre, up_pre, down_weight
+    )
+    squares = jnp.sum(norm)
+    entry_count = (
+        float(experts_here * lax.axis_size("expert"))
+        * float(hidden_width * n_dp)
+        * float(feature_width * lax.axis_size("ffn"))
+    )
+    clip_limit = jnp.float32(0.5 * math.sqrt(entry_count))
+    factor = clip_limit / jnp.maximum(jnp.sqrt(squares), clip_limit)
+    down_grad = (wide.astype(F32) * factor).astype(BF16)
+    return (down_grad, gate_grad, up_grad)
+
+
 def solution(mesh):
     placed = (
         P("dp", "ffn"),
@@ -80,8 +504,9 @@
         P("expert", "ffn", "dp"),
         P("expert", "dp", "ffn"),
     )
+    fits = mesh.shape["dp"] == 8 and mesh.shape["expert"] == 2 and mesh.shape["ffn"] == 2
     return jax.shard_map(
-        on_device,
+        fused_device if fits else on_device,
         mesh=mesh,
         in_specs=placed,
         out_specs=(P("expert", "dp", "ffn"), P("expert", "ffn", "dp"), P("expert", "ffn", "dp")),

time: 296 us -> 105 us (0.35)
  waiting for transfers between devices: 181 us -> 0 us
  Pallas kernels: 0 us -> 86.8 us
  blocking collectives: 39.5 us -> 0 us
  matrix products: 36.8 us -> 0 us
  between operations: 14.5 us -> 1.4 us
  other arithmetic: 21.4 us -> 14.9 us
    all_gather x2 -> x0, waiting for transfers between devices: 148 us -> none  [the longest x1 112 us: on_device(): arrived = lax.all_gather(dispatched, 'dp', axis=1, tiled=True)]
    pallas_call x0 -> x1, Pallas kernels: none -> 86.8 us  [fused_call(): pl.pallas_call(functools.partial(fused_kernel, n_dp), out_shape=(jax.Shap...]
    psum x1 -> x0, blocking collectives: 39.5 us -> none  [on_device(): lax.psum(jnp.sum(weight_grad * weight_grad), ('dp', 'expert', 'ffn'))]
    dot_general x4 -> x0, matrix products: 36.8 us -> none  [the longest x1 20.4 us: on_device(): jnp.einsum('erf,erd->efd', lax.all_gather(hidden, 'ffn', axis=1, tiled=Tr...]
    reduce_scatter x1 -> x0, waiting for transfers between devices: 32.8 us -> none  [on_device(): lax.psum_scatter(partial_sums.astype(jnp.bfloat16), 'ffn', scatter_dimens...]
    convert_element_type x3 -> x2, other arithmetic: 19.4 us -> 12.3 us  [the longest x1 11.6 us: fused_device(): down_grad = (wide.astype(F32) * factor).astype(BF16)]
  transfers between devices with their start and end apart: 3 -> 0, of which waited for: 3 -> 0; matrix products, arithmetic and copies ran while one was open for 0% -> 0% of each run, Pallas kernels for 0% -> 0%
where the time goes in v1:
time: 105 us
  Pallas kernels  86.8 us (83%)
  other arithmetic  14.9 us (14%)
  local copies, waits for them, and re-layouts  2.11 us (2%)
  between operations  1.4 us (1%)
    pallas_call x1, Pallas kernels, fused_call(): pl.pallas_call(functools.partial(fused_kernel, n_dp), out_shape=(jax.Shap...  86.8 us
    convert_element_type x1, other arithmetic, fused_device(): down_grad = (wide.astype(F32) * factor).astype(BF16)  11.6 us

profile of v1, /device:TPU:0, one launch (start us, length us, event | category | flops | bytes accessed | tf_op | source)
XLA Modules:
  0.0 105.2 jit_solution(159588354080869535)
XLA Ops:
  0.6 0.1 pad.2.clone
  0.7 0.7 convert_element_type.9
  1.4 1.3 %maximum_bitcast_fusion.meta_ref = f32[8,128]{1,0:T(8,128)} fusion(f32[128,2]{0,1:T(2,128)} %param.7, f32[128,2]{0,1:T(2,128)S(1)} %convert_element_type.9, f32[8]{0:T(128)S(1)} %pad.2.clone), kind=kLoop, calls=%fused_computation.1 | loop fusion | flops 2048 | bytes 6176 | tf_op jit(solution)/shard_map/transpose | solution.py:482
  2.7 86.8 %shard_map.85 = (bf16[2,1024,3072]{2,1,0:T(8,128)(2,1)}, bf16[2,288,1024]{2,1,0:T(8,128)(2,1)}, bf16[2,288,1024]{2,1,0:T(8,128)(2,1)}, f32[8,128]{1,0:T(8,128)}) custom-call(f32[8,128]{1,0:T(8,128)} %maximum_bitcast_fusion.meta_ref, bf16[128,3072]{1,0:T(8,128)(2,1)} %rows_ref.1, bf16[2,288,1024]{2,1,0:T(8,128)(2,1)} %gate_ref.1, ...), custom_call_target="tpu_custom_call" | custom-call | tf_op jit(solution)/shard_map/pallas_call | solution.py:428
  89.5 1.3 %reduce_sum.9 = f32[]{:T(128)} reduce(f32[8,128]{1,0:T(8,128)} %get-tuple-element.8, f32[]{:T(128)} %constant.2.clone.1), dimensions={0,1}, to_apply=%region_0.0 | reduce | flops 1023 | bytes 4104 | tf_op jit(solution)/shard_map/reduce_sum | solution.py:486
  91.6 0.0 copy-start.1
  91.6 0.0 copy-start
  91.6 11.6 %multiply_convert_fusion = bf16[2,1024,3072]{2,1,0:T(8,128)(2,1)} fusion(bf16[2,1024,3072]{2,1,0:T(8,128)(2,1)} %get-tuple-element.7, f32[]{:T(128)S(6)} %div.3), kind=kLoop, calls=%fused_computation | loop fusion | flops 18874368 | bytes 25165828 | tf_op jit(solution)/shard_map/convert_element_type | solution.py:494
  103.2 0.0 copy-done.1
  103.2 1.0 copy.11
  104.2 0.0 copy-done
  104.2 1.0 copy.12
  (1 shorter events, 0.0 us)
Async XLA Ops:
  91.6 11.6 %copy-start.1 = (bf16[2,288,1024]{2,1,0:T(8,128)(2,1)S(1)}, bf16[2,288,1024]{2,1,0:T(8,128)(2,1)}, u32[]{:S(2)}) copy-start(bf16[2,288,1024]{2,1,0:T(8,128)(2,1)} %get-tuple-element.15) | copy-start | bytes 3538948
  91.6 12.6 %copy-start = (bf16[2,288,1024]{2,1,0:T(8,128)(2,1)S(1)}, bf16[2,288,1024]{2,1,0:T(8,128)(2,1)}, u32[]{:S(2)}) copy-start(bf16[2,288,1024]{2,1,0:T(8,128)(2,1)} %get-tuple-element.16) | copy-start | bytes 3538948

commit v2 on v1

--- a/solution.py
+++ b/solution.py
@@ -78,12 +78,12 @@
 
 
 def fused_kernel(
-    n_dp, meta_ref, rows_ref, gate_ref, up_ref, weight_ref,
-    wide_ref, gate_out, up_out, norm_ref,
-    tokens, metas, placed, weight, hidden, hidden_t, mine, outgoing, incoming,
+    n_dp, ids_ref, probs_ref, rows_ref, gate_ref, up_ref, weight_ref,
+    placed_out, hidden_out, mine_out, incoming, norm_ref,
+    tokens, metas, placed, weight, hidden, hidden_t, mine, outgoing,
     squares, norm_dp, norm_core, norm_pair, own_norm,
     load_sem, meta_send, meta_recv, z_send, z_recv, x_send, x_recv, core_send, core_recv,
-    hidden_send, hidden_recv, part_send, part_recv, norm_send, norm_recv, wide_sem,
+    hidden_send, hidden_recv, part_send, part_recv, norm_send, norm_recv, store_sem,
 ):
     dp = lax.axis_index("dp")
     core = lax.axis_index("expert")
@@ -144,7 +144,9 @@
             {"dp": (dp + step) % n_dp},
         )
 
-    metas[dp] = meta_ref[...]
+    metas[dp] = jnp.concatenate(
+        [ids_ref[...].astype(F32), probs_ref[...], jnp.zeros((4, block), F32)], axis=0
+    )
     for step in range(1, n_dp):
         meta_copy(step, dp).start()
     load_rows.wait()
@@ -188,8 +190,9 @@
     unit_cols = 256
 
     def part_copy(index, e):
+        at = pl.ds(pl.multiple_of(index * group, 16), group)
         return remote(
-            outgoing.at[index, e], incoming.at[index, e], part_send.at[index, e],
+            outgoing.at[e, at, :], incoming.at[e, at, :], part_send.at[index, e],
             part_recv.at[index, e], {"ffn": 1 - side},
         )
 
@@ -228,6 +231,7 @@
             lax.fori_loop(0, n_cols, place_cols, 0)
         is_own = (g // groups_own) == side
         index = g % groups_own
+        index_rows = pl.ds(pl.multiple_of(index * group, 16), group)
         for e in range(experts):
 
             def unit_tile(j, carry):
@@ -239,11 +243,11 @@
 
                 @pl.when(is_own)
                 def _():
-                    mine[index, e, :, at] = term
+                    mine[e, index_rows, at] = term
 
                 @pl.when(jnp.logical_not(is_own))
                 def _():
-                    outgoing[index, e, :, at] = term
+                    outgoing[e, index_rows, at] = term
 
                 return carry
 
@@ -296,10 +300,48 @@
 
     lax.fori_loop(0, n_z, stage, 0)
 
+    store_placed = pltpu.make_async_copy(placed, placed_out, store_sem.at[0])
+    store_placed.start()
+    store_mine = pltpu.make_async_copy(mine, mine_out, store_sem.at[1])
+    store_mine.start()
     for e in range(experts):
         hidden_copy(e, 1 - side).wait_recv()
         hidden_copy(e, side).wait_send()
+
+    squares[...] = jnp.zeros_like(squares)
     slots = hidden.shape[1]
+    part = slots // 2
+    contract = (((1,), (1,)), ((), ()))
+
+    def add_squares(e, carry):
+        for a, b in ((0, 0), (0, 1), (1, 1)):
+            left, right = pl.ds(a * part, part), pl.ds(b * part, part)
+            rows_product = lax.dot_general(
+                placed[e, left, :], placed[e, right, :], contract, preferred_element_type=F32
+            )
+            hidden_product = lax.dot_general(
+                hidden[e, left, :], hidden[e, right, :], contract, preferred_element_type=F32
+            )
+            both = rows_product * hidden_product
+            if a != b:
+                both = both + both
+            folded = jnp.sum(both.reshape(part // 8, 8, part), axis=0)
+            squares[...] += jnp.broadcast_to(jnp.sum(folded, axis=1, keepdims=True), (8, 128))
+        return carry
+
+    lax.fori_loop(0, experts, add_squares, 0)
+
+    own_norm[0] = squares[...]
+
+    def norm_copy(step, to_slot):
+        return remote(
+            own_norm.at[0], norm_dp.at[to_slot], norm_send.at[step], norm_recv.at[step],
+            {"dp": (dp + step) % n_dp},
+        )
+
+    for step in range(1, n_dp):
+        norm_copy(step, dp).start()
+    norm_dp[dp] = own_norm[0]
     for e in range(experts):
 
         def turn(j, carry):
@@ -308,38 +350,8 @@
             return carry
 
         lax.fori_loop(0, units // 128, turn, 0)
-
-    squares[...] = jnp.zeros_like(squares)
-    tile = 256
-    tiles = width // tile
-
-    def wide_copy(e, j):
-        at = pl.ds(pl.multiple_of(j * tile, 128), tile)
-        return pltpu.make_async_copy(weight.at[e, :, at], wide_ref.at[e, :, at], wide_sem.at[e, j])
-
-    for e in range(experts):
-
-        def wide_tile(j, carry):
-            at = pl.ds(pl.multiple_of(j * tile, 128), tile)
-            product = jnp.dot(hidden_t[e], placed[e, :, at], preferred_element_type=F32)
-            weight[e, :, at] = product.astype(BF16)
-            squares[...] += jnp.sum((product * product).reshape(units // 8, 8, tile), axis=0)
-            wide_copy(e, j).start()
-            return carry
-
-        lax.fori_loop(0, tiles, wide_tile, 0)
-
-    own_norm[0] = squares[:, 0:128] + squares[:, 128:256]
-
-    def norm_copy(step, to_slot):
-        return remote(
-            own_norm.at[0], norm_dp.at[to_slot], norm_send.at[step], norm_recv.at[step],
-            {"dp": (dp + step) % n_dp},
-        )
-
-    for step in range(1, n_dp):
-        norm_copy(step, dp).start()
-    norm_dp[dp] = own_norm[0]
+    store_hidden = pltpu.make_async_copy(hidden_t, hidden_out, store_sem.at[2])
+    store_hidden.start()
     for step in range(1, n_dp):
         norm_copy(step, (dp - step + n_dp) % n_dp).wait_recv()
     total = norm_dp[0]
@@ -357,32 +369,12 @@
     )
     pair_norm.start()
 
+    pair_norm.wait()
+    norm_ref[...] = own_norm[2] + norm_pair[...]
+
     for index in range(groups_own):
         for e in range(experts):
-            part_copy(index, e).wait_recv()
-
-            def grad_piece(i, carry):
-                here = pl.multiple_of(i * piece, 16)
-                at = pl.ds(pl.multiple_of(index * group + here, 16), piece)
-                gate = gate_ref[e, at, :].astype(F32)
-                up = up_ref[e, at, :].astype(F32)
-                grad = (
-                    mine[index, e, pl.ds(here, piece), :].astype(F32)
-                    + incoming[index, e, pl.ds(here, piece), :].astype(F32)
-                )
-                sig = jax.nn.sigmoid(gate)
-                gate_out[e, at, :] = (grad * up * sig * (1.0 + gate * (1.0 - sig))).astype(BF16)
-                up_out[e, at, :] = (grad * (gate * sig)).astype(BF16)
-                return carry
-
-            lax.fori_loop(0, group // piece, grad_piece, 0)
-
-    pair_norm.wait()
-    norm_ref[...] = own_norm[2] + norm_pair[...]
-
-    for index in range(groups_own):
-        for e in range(experts):
-            part_copy(index, e).wait_send()
+            part_copy(index, e).wait()
     for step in range(1, n_dp):
         meta_copy(step, dp).wait_send()
         norm_copy(step, dp).wait_send()
@@ -406,20 +398,15 @@
         return carry
 
     lax.fori_loop(0, n_z, drain, 0)
-    for e in range(experts):
-
-        def wide_wait(j, carry):
-            wide_copy(e, j).wait()
-            return carry
-
-        lax.fori_loop(0, tiles, wide_wait, 0)
-
-
-def fused_call(n_dp, meta, grad_rows, gate_pre, up_pre, down_weight):
+    store_placed.wait()
+    store_mine.wait()
+    store_hidden.wait()
+
+
+def fused_call(n_dp, ids, probs, grad_rows, gate_pre, up_pre, down_weight):
     experts, own_slots, units = gate_pre.shape
     block, width = grad_rows.shape
     n_z = n_dp // 2
-    group = 2 * CAP
     groups_own = n_z // 2
     slots = n_dp * CAP
     vmem = pl.BlockSpec(memory_space=pltpu.VMEM)
@@ -428,13 +415,14 @@
     return pl.pallas_call(
         functools.partial(fused_kernel, n_dp),
         out_shape=(
-            jax.ShapeDtypeStruct(down_weight.shape, BF16),
+            jax.ShapeDtypeStruct((experts, slots, width), BF16),
+            jax.ShapeDtypeStruct((experts, units, slots), BF16),
             jax.ShapeDtypeStruct(gate_pre.shape, BF16),
-            jax.ShapeDtypeStruct(up_pre.shape, BF16),
+            jax.ShapeDtypeStruct(gate_pre.shape, BF16),
             jax.ShapeDtypeStruct((8, 128), F32),
         ),
-        in_specs=[vmem, hbm, vmem, vmem, hbm],
-        out_specs=(hbm, vmem, vmem, vmem),
+        in_specs=[vmem, vmem, hbm, vmem, vmem, hbm],
+        out_specs=(hbm, hbm, hbm, hbm, vmem),
         scratch_shapes=[
             pltpu.VMEM((n_z, 2 * block, width), BF16),
             pltpu.VMEM((n_dp, 8, block), F32),
@@ -442,10 +430,9 @@
             pltpu.VMEM(down_weight.shape, BF16),
             pltpu.VMEM((experts, slots, units), BF16),
             pltpu.VMEM((experts, units, slots), BF16),
-            pltpu.VMEM((groups_own, experts, group, units), BF16),
-            pltpu.VMEM((groups_own, experts, group, units), BF16),
-            pltpu.VMEM((groups_own, experts, group, units), BF16),
-            pltpu.VMEM((8, 256), F32),
+            pltpu.VMEM(gate_pre.shape, BF16),
+            pltpu.VMEM(gate_pre.shape, BF16),
+            pltpu.VMEM((8, 128), F32),
             pltpu.VMEM((n_dp, 8, 128), F32),
             pltpu.VMEM((8, 128), F32),
             pltpu.VMEM((8, 128), F32),
@@ -465,34 +452,67 @@
             dma((groups_own, experts)),
             dma((n_dp + 1,)),
             dma((n_dp + 1,)),
-            dma((experts, width // 256)),
+            dma((3,)),
         ],
         compiler_params=pltpu.CompilerParams(
             collective_id=0, has_side_effects=True, vmem_limit_bytes=58 * 1024 * 1024
         ),
-    )(meta, grad_rows, gate_pre, up_pre, down_weight)
+    )(ids, probs, grad_rows, gate_pre, up_pre, down_weight)
+
+
+def finish_kernel(
+    clip_limit, norm_ref, hidden_ref, placed_ref, gate_ref, up_ref, mine_ref, theirs_ref,
+    wide_out, gate_out, up_out,
+):
+    squares = jnp.sum(jnp.sum(norm_ref[...], axis=0, keepdims=True), axis=1, keepdims=True) / 128.0
+    factor = clip_limit / jnp.maximum(jnp.sqrt(squares), clip_limit)
+    product = jnp.dot(hidden_ref[0], placed_ref[0], preferred_element_type=F32)
+    wide_out[0] = (product * factor).astype(BF16)
+    gate = gate_ref[0].astype(F32)
+    up = up_ref[0].astype(F32)
+    grad = mine_ref[0].astype(F32) + theirs_ref[0].astype(F32)
+    sig = jax.nn.sigmoid(gate)
+    gate_out[0] = (grad * up * sig * (1.0 + gate * (1.0 - sig))).astype(BF16)
+    up_out[0] = (grad * (gate * sig)).astype(BF16)
+
+
+def finish_call(clip_limit, norm, hidden_t, placed, gate_pre, up_pre, mine, theirs):
+    experts, units, slots = hidden_t.shape
+    width = placed.shape[2]
+    steps = 6
+    tile, piece = width // steps, gate_pre.shape[1] // steps
+    rows = pl.BlockSpec((1, piece, units), lambda e, j: (e, j, 0))
+    return pl.pallas_call(
+        functools.partial(finish_kernel, clip_limit),
+        grid=(experts, steps),
+        out_shape=(
+            jax.ShapeDtypeStruct((experts, units, width), BF16),
+            jax.ShapeDtypeStruct(gate_pre.shape, BF16),
+            jax.ShapeDtypeStruct(gate_pre.shape, BF16),
+        ),
+        in_specs=[
+            pl.BlockSpec((8, 128), lambda e, j: (0, 0)),
+            pl.BlockSpec((1, units, slots), lambda e, j: (e, 0, 0)),
+            pl.BlockSpec((1, slots, tile), lambda e, j: (e, 0, j)),
+            rows, rows, rows, rows,
+        ],
+        out_specs=(pl.BlockSpec((1, units, tile), lambda e, j: (e, 0, j)), rows, rows),
+        compiler_params=pltpu.CompilerParams(vmem_limit_bytes=60 * 1024 * 1024),
+    )(norm, hidden_t, placed, gate_pre, up_pre, mine, theirs)
 
 
 def fused_device(grad_rows, gate_probs, expert_ids, gate_pre, up_pre, down_weight):
-    experts_here, rows_here, hidden_width = gate_pre.shape
-    feature_width = down_weight.shape[2]
     n_dp = lax.axis_size("dp")
-    meta = jnp.concatenate(
-        [expert_ids.astype(F32), gate_probs, jnp.zeros((expert_ids.shape[0], 4), F32)], axis=1
-    ).T
-    wide, gate_grad, up_grad, norm = fused_call(
-        n_dp, meta, grad_rows, gate_pre, up_pre, down_weight
-    )
-    squares = jnp.sum(norm)
     entry_count = (
-        float(experts_here * lax.axis_size("expert"))
-        * float(hidden_width * n_dp)
-        * float(feature_width * lax.axis_size("ffn"))
-    )
-    clip_limit = jnp.float32(0.5 * math.sqrt(entry_count))
-    factor = clip_limit / jnp.maximum(jnp.sqrt(squares), clip_limit)
-    down_grad = (wide.astype(F32) * factor).astype(BF16)
-    return (down_grad, gate_grad, up_grad)
+        float(gate_pre.shape[0] * lax.axis_size("expert"))
+        * float(gate_pre.shape[2] * n_dp)
+        * float(down_weight.shape[2] * lax.axis_size("ffn"))
+    )
+    clip_limit = 0.5 * math.sqrt(entry_count)
+    placed, hidden_t, mine, theirs, norm = fused_call(
+        n_dp, expert_ids.T, gate_probs.T, grad_rows, gate_pre, up_pre, down_weight
+    )
+    return finish_call(clip_limit, norm, hidden_t, placed, gate_pre, up_pre, mine, theirs)
 
 
 def solution(mesh):

time: 105 us -> 97.5 us (0.929)
  other arithmetic: 14.9 us -> 0 us
  Pallas kernels: 86.8 us -> 96.4 us
  local copies, waits for them, and re-layouts: 2.11 us -> 0 us
    pallas_call x0 -> x1, Pallas kernels: none -> 18.7 us  [finish_call(): pl.pallas_call(functools.partial(finish_kernel, clip_limit), grid=(expert...]
    convert_element_type x2 -> x0, other arithmetic: 12.3 us -> none  [the longest x1 11.6 us: fused_device(): down_grad = (wide.astype(F32) * factor).astype(BF16)]
    pallas_call x1, Pallas kernels: 86.8 us -> 77.8 us  [fused_call(): pl.pallas_call(functools.partial(fused_kernel, n_dp), out_shape=(jax.Shap...]
    unnamed x6 -> x0, local copies, waits for them, and re-layouts: 2.03 us -> none
    transpose x1 -> x0, other arithmetic: 1.34 us -> none  [fused_device(): meta = jnp.concatenate([expert_ids.astype(F32), gate_probs, jnp.zeros((ex...]
    reduce_sum x1 -> x0, other arithmetic: 1.29 us -> none  [fused_device(): squares = jnp.sum(norm)]
where the time goes in v2:
time: 97.5 us; the launch traced here: 97.1 us
  Pallas kernels  96.4 us (99%)
    pallas_call x1, Pallas kernels, fused_call(): pl.pallas_call(functools.partial(fused_kernel, n_dp), out_shape=(jax.Shap...  77.8 us
    pallas_call x1, Pallas kernels, finish_call(): pl.pallas_call(functools.partial(finish_kernel, clip_limit), grid=(expert...  18.7 us

profile of v2, /device:TPU:0, one launch (start us, length us, event | category | flops | bytes accessed | tf_op | source)
XLA Modules:
  0.0 97.1 jit_solution(12514967019219501848)
XLA Ops:
  0.6 77.8 %shard_map.85 = (bf16[2,576,3072]{2,1,0:T(8,128)(2,1)}, bf16[2,1024,576]{2,1,0:T(8,128)(2,1)}, bf16[2,288,1024]{2,1,0:T(8,128)(2,1)}, bf16[2,288,1024]{2,1,0:T(8,128)(2,1)}, f32[8,128]{1,0:T(8,128)}) custom-call(s32[2,128]{1,0:T(2,128)} %bitcast.2, f32[2,128]{1,0:T(2,128)} %bitcast.3, bf16[128,3072]{1,0:T(8,128)(2,1)} %rows_ref.1, ...), custom_call_target="tpu_custom_call" | custom-call | tf_op jit(solution)/shard_map/pallas_call | solution.py:415
  78.4 18.7 %shard_map.86 = (bf16[2,1024,3072]{2,1,0:T(8,128)(2,1)}, bf16[2,288,1024]{2,1,0:T(8,128)(2,1)}, bf16[2,288,1024]{2,1,0:T(8,128)(2,1)}) custom-call(f32[8,128]{1,0:T(8,128)} %get-tuple-element.8.norm_ref, bf16[2,1024,576]{2,1,0:T(8,128)(2,1)} %get-tuple-element.9.hidden_ref, bf16[2,576,3072]{2,1,0:T(8,128)(2,1)} %get-tuple-element.10.placed_ref, ...), custom_call_target="tpu_custom_call" | custom-call | tf_op jit(solution)/shard_map/pallas_call | solution.py:485
